TPU v7x, 512 devices: a whole 4x8x8 slice. The times are simulated.
512 devices in a mesh: row: 32 (over x_hi, z, core), col: 16 (over x_lo, y).
Axes of the slice: x: 4 (x_hi: 2, x_lo: 2; x = x_hi * 2 + x_lo), y: 8, z: 8, core: 2. Of those that a mesh axis runs over, the one named last changes fastest.
Arguments:
- pair: bfloat16 [512, 512, 128], P('row', 'col'), may hold values from -6 to 6
- pair_mask: int32 [512, 512], P('row', 'col'), may hold values 0 or 1
- in_weights: bfloat16 [128, 512], replicated, may hold values from -0.5 to 0.5
- gate_weight: bfloat16 [128, 128], replicated, may hold values from -0.5 to 0.5
- out_weight: bfloat16 [128, 128], replicated, may hold values from -0.5 to 0.5
Outputs:
- update: bfloat16 [512, 512, 128], P('row', 'col')
All inputs are finite; a program needn't handle non-finite values. No bound on the sum of `pair_mask` on one device may be relied on, other than what follows from the above.
Results may differ from a plain program's by a relative error of at most 0.0078.
Values may be sent and summed in bfloat16 or wider, within the bound.
A program may use at most 64 MiB of HBM per device.

v0:
```python
import jax
import jax.numpy as jnp
from jax import lax
from jax.sharding import PartitionSpec as P


def spread(value, axis, root):
    mine = lax.axis_index(axis) == root
    return lax.psum(jnp.where(mine, value, jnp.zeros_like(value)), axis)


def layer_norm(values):
    mean = jnp.mean(values, axis=-1, keepdims=True)
    centred = values - mean
    var = jnp.mean(centred * centred, axis=-1, keepdims=True)
    return centred * jax.lax.rsqrt(var + 1e-05)


def body(pair, pair_mask, in_weights, gate_weight, out_weight):
    rows_here = pair.shape[0]
    cols_here = pair.shape[1]
    width = pair.shape[2]
    hidden = in_weights.shape[1] // 4
    normed = layer_norm(pair.reshape(-1, width).astype(jnp.float32)).astype(jnp.bfloat16)
    proj = jnp.dot(normed, in_weights, preferred_element_type=jnp.float32)
    maskf = pair_mask.reshape(-1, 1).astype(jnp.float32)
    left = (maskf * jax.nn.sigmoid(proj[:, hidden : 2 * hidden]) * proj[:, :hidden]).astype(
        jnp.bfloat16
    )
    right = (
        maskf * jax.nn.sigmoid(proj[:, 3 * hidden :]) * proj[:, 2 * hidden : 3 * hidden]
    ).astype(jnp.bfloat16)
    left = left.reshape(rows_here, cols_here, hidden)
    right = right.reshape(rows_here, cols_here, hidden)
    gate = jax.nn.sigmoid(jnp.dot(normed, gate_weight, preferred_element_type=jnp.float32))
    ratio = lax.axis_size("row") // lax.axis_size("col")
    column = lax.axis_index("col")
    left_rows, right_rows = (
        lax.all_gather(left, "col", axis=1, tiled=True),
        lax.all_gather(right, "col", axis=1, tiled=True),
    )
    blocks = [spread(right_rows, "row", ratio * column + offset) for offset in range(ratio)]
    partner = jnp.concatenate(blocks, axis=0)
    tri = jnp.einsum("ikc,jkc->ijc", left_rows, partner, preferred_element_type=jnp.float32)
    tnorm = layer_norm(tri.reshape(-1, hidden)).astype(jnp.bfloat16)
    update = gate * jnp.dot(tnorm, out_weight, preferred_element_type=jnp.float32)
    return update.astype(jnp.bfloat16).reshape(rows_here, cols_here, width)


def solution(mesh):
    in_specs = (P("row", "col", None), P("row", "col"), P(), P(), P())
    out_specs = P("row", "col", None)
    return jax.shard_map(body, mesh=mesh, in_specs=in_specs, out_specs=out_specs, check_vma=False)
```

profile of v0, /device:TPU:1, one launch (start us, length us, event | category | flops | bytes accessed | tf_op | source)
XLA Modules:
  0.0 462.7 jit_solution(1280969838213901515)
XLA Ops:
  6.5 0.0 copy-start
  6.5 0.0 all-gather.3.cloned.1.call-start
  6.5 1.1 convert_reduce_fusion
  7.6 1.2 multiply_reduce_fusion.1
  8.8 0.1 div.26
  8.9 0.1 rsqrt.23
  9.0 0.7 convert_element_type.40
  9.7 0.1 convert_element_type.41
  9.8 1.1 fusion.24
  10.9 0.0 copy-done
  10.9 0.3 fusion.27
  11.2 0.2 fusion.16
  11.3 0.7 copy.11
  12.0 0.0 all-gather.3.cloned.1.call-update
  12.1 0.0 all-gather.5.cloned.1.call-start
  12.1 0.7 copy.14
  12.8 0.0 all-gather.5.cloned.1.call-update
  12.8 0.0 all-reduce.3.cloned.1.call-start
  12.9 69.3 %all-gather.3.cloned.1.call-done = bf16[16,512,128]{2,0,1:T(8,128)(2,1)} async-done(((bf16[16,32,128]{2,0,1:T(8,128)(2,1)}), bf16[16,512,128]{2,0,1:T(8,128)(2,1)}) %all-gather.3.cloned.1.call-update) | async-done | bytes 2097168 | tf_op jit(solution)/shard_map/all_gather | solution.py:40
  82.2 3.9 copy.12
  86.1 2.3 broadcast_select_fusion.1
  88.4 0.0 copy-start.2
  88.4 0.0 all-reduce.3.cloned.1.call-update
  88.4 0.7 copy-done.2
  89.2 0.2 fusion.9
  89.4 66.4 %all-gather.5.cloned.1.call-done = bf16[16,512,128]{2,0,1:T(8,128)(2,1)} async-done(((bf16[16,32,128]{2,0,1:T(8,128)(2,1)}), bf16[16,512,128]{2,0,1:T(8,128)(2,1)}) %all-gather.5.cloned.1.call-update) | async-done | bytes 2097168 | tf_op jit(solution)/shard_map/all_gather | solution.py:39
  155.8 3.9 copy.15
  159.7 291.1 %all-reduce.3.cloned.1.call-done = (bf16[16,512,128]{1,0,2:T(8,128)(2,1)}, bf16[16,512,128]{1,0,2:T(8,128)(2,1)}) async-done(((bf16[16,512,128]{1,0,2:T(8,128)(2,1)}, bf16[16,512,128]{1,0,2:T(8,128)(2,1)}), (bf16[16,512,128]{1,0,2:T(8,128)(2,1)}, bf16[16,512,128]{1,0,2:T(8,128)(2,1)})) %all-reduce.3.cloned.1.call-update) | async-done | bytes 4194320 | tf_op jit(solution)/shard_map/psum | solution.py:9
  450.9 3.4 fusion.26
  454.3 0.0 copy-start.1
  454.3 0.4 copy.16
  454.7 0.2 multiply_reduce_fusion
  454.9 0.1 div.32
  455.0 0.1 rsqrt.25
  455.1 0.2 fusion.22
  455.3 0.0 copy-done.1
  455.3 0.8 fusion.10
  (4 shorter events, 0.0 us)
Async XLA Ops:
  6.5 4.3 copy-start
  6.5 75.7 %all-gather.3.cloned.1.call-start = ((), (), s32[]{:S(2)}) async-start(), calls=%async_computation | async-start | bytes 2228224 | tf_op jit(solution)/shard_map/all_gather | solution.py:40
  12.1 143.7 %all-gather.5.cloned.1.call-start = ((), (), s32[]{:S(2)}) async-start(), calls=%async_computation.1 | async-start | bytes 2228224 | tf_op jit(solution)/shard_map/all_gather | solution.py:39
  12.8 438.0 %all-reduce.3.cloned.1.call-start = ((), (), s32[]{:S(2)}) async-start(), calls=%async_computation.2 | async-start | bytes 8388608 | tf_op jit(solution)/shard_map/psum | solution.py:9
  88.4 0.8 copy-start.2
  454.3 1.0 copy-start.1
Sparse Core Ops, SparseCore 0:
  12.2 69.9 all-gather.2
  84.3 71.4 all-gather.4
  158.8 292.0 all-reduce.2
where the time goes:
time: 463 us
  waiting for transfers between devices  427 us (92%)
  between operations  13.2 us (3%)
  local copies, waits for them, and re-layouts  10.8 us (2%)
  other arithmetic  6.94 us (1%)
  matrix products  4.75 us (1%)
    psum x1, waiting for transfers between devices, spread(): return lax.psum(jnp.where(mine, value, jnp.zeros_like(value)), axis)  291 us
    all_gather x1, waiting for transfers between devices, body(): lax.all_gather(right, 'col', axis=1, tiled=True)  69.3 us
    all_gather x1, waiting for transfers between devices, body(): lax.all_gather(left, 'col', axis=1, tiled=True)  66.4 us
  transfers between devices with their start and end apart: 3, of which 3 were waited for; matrix products, arithmetic and copies ran while one was open for 2% of the time, Pallas kernels for 0%

commit v1 on v0

v1 whole, which is shorter than its diff:
```python
import jax
import jax.numpy as jnp
from jax import lax
from jax.experimental import pallas as pl
from jax.experimental.pallas import tpu as pltpu
from jax.sharding import PartitionSpec as P

MESH = pl.DeviceIdType.MESH
F32 = jnp.float32
BF16 = jnp.bfloat16

ROWS, COLS = 32, 16
NZ = 8
IL, KL = 16, 32
N = 512
POS = IL * KL
C = 128


def layer_norm(values, axis):
    mean = jnp.mean(values, axis=axis, keepdims=True)
    centred = values - mean
    var = jnp.mean(centred * centred, axis=axis, keepdims=True)
    return centred * lax.rsqrt(var + 1e-05)


def sigmoid(x):
    return 0.5 * jnp.tanh(0.5 * x) + 0.5


def swap_blocks(v):
    lane = lax.broadcasted_iota(jnp.int32, v[0].shape, 1)
    low64 = lane < 64
    low32 = (lane % 64) < 32
    a = [None] * 4
    for c in range(2):
        a[c] = jnp.where(low64, v[c], pltpu.roll(v[c + 2], 64, 1))
        a[c + 2] = jnp.where(low64, pltpu.roll(v[c], 64, 1), v[c + 2])
    out = [None] * 4
    for h in (0, 2):
        out[h] = jnp.where(low32, a[h], pltpu.roll(a[h + 1], 32, 1))
        out[h + 1] = jnp.where(low32, pltpu.roll(a[h], 96, 1), a[h + 1])
    return out


def kernel(
    pair_hbm, mask_hbm, w_hbm, gw_hbm, ow_hbm, out_ref,
    pair_ref, mask_ref, w_ref, gw_ref, ow_ref,
    proj, gate, send1, recv1, turn, send2, recv_l, recv_r, send3, recv3, wide3, send4, recv4,
    load_sem, s1, r1, s2, r2l, r2r, s3, r3, s4, r4,
):
    r, c = lax.axis_index("row"), lax.axis_index("col")
    xh, z, core = r // 16, (r // 2) % NZ, r % 2
    zc = r % 16

    loads = []
    for n, (src, dst) in enumerate(
        ((pair_hbm, pair_ref), (mask_hbm, mask_ref), (w_hbm, w_ref), (gw_hbm, gw_ref), (ow_hbm, ow_ref))
    ):
        loads.append(pltpu.make_async_copy(src, dst, load_sem.at[n]))
        loads[-1].start()

    barrier = pltpu.get_barrier_semaphore()

    @pl.loop(1, COLS)
    def _(d):
        pl.semaphore_signal(barrier, inc=1, device_id=(r, (c + d) % COLS), device_id_type=MESH)

    @pl.loop(1, ROWS)
    def _(d):
        pl.semaphore_signal(barrier, inc=1, device_id=((r + d) % ROWS, c), device_id_type=MESH)

    for load in loads:
        load.wait()

    normed = layer_norm(pair_ref[...].reshape(POS, C).astype(F32), 1)
    eye = lax.broadcasted_iota(jnp.int32, (KL, KL), 0) == lax.broadcasted_iota(jnp.int32, (KL, KL), 1)
    maskf = mask_ref[...].astype(F32)
    column = jnp.concatenate(
        [jnp.sum(jnp.where(eye, maskf[il : il + 1, :], 0.0), axis=1, keepdims=True) for il in range(IL)], axis=0
    )
    masked = (normed * column).astype(BF16)
    normed = normed.astype(BF16)
    proj[...] = lax.dot_general(w_ref[...], masked, (((0,), (1,)), ((), ())), preferred_element_type=F32)

    pl.semaphore_wait(barrier, COLS + ROWS - 2)

    def operands(g):
        at = [pl.ds(pl.multiple_of(block * C + g * 8, 8), 8) for block in range(4)]
        left = sigmoid(proj[at[1], :]) * proj[at[0], :]
        right = sigmoid(proj[at[3], :]) * proj[at[2], :]
        return jnp.concatenate([left, right], axis=0).astype(BF16)

    @pl.loop(1, COLS)
    def _(d):
        g = (c + d) % COLS
        send1[g] = operands(g)
        pltpu.make_async_remote_copy(send1.at[g], recv1.at[c], s1.at[d], r1.at[c], (r, g), MESH).start()

    recv1[c] = operands(c)
    gate[...] = sigmoid(jnp.dot(normed, gw_ref[...], preferred_element_type=F32))

    @pl.loop(1, COLS)
    def _(d):
        g = (c + d) % COLS
        pltpu.make_async_copy(recv1.at[g], recv1.at[g], r1.at[g]).wait()

    for b in range(4):
        for a in range(4):
            tiles = [recv1[4 * a + q, :, 128 * b : 128 * b + 128].astype(F32) for q in range(4)]
            for q, tile in enumerate(swap_blocks(tiles)):
                row = 256 * a + 16 * (4 * b + q)
                turn[row : row + 16, :] = tile
    for m in range(16):
        for a in range(4):
            send2[m, :, 128 * a : 128 * a + 128] = turn[pl.ds(256 * a + m, 16, stride=16), :].astype(BF16)

    def put2(n, src, dst, rsem, to):
        pltpu.make_async_remote_copy(src, dst.at[zc], s2.at[n], rsem.at[zc], (to, c), MESH).start()

    @pl.loop(1, NZ)
    def _(d):
        e = (z + d) % NZ
        for k in range(2):
            put2(4 * d + k, send2.at[e], recv_l, r2l, xh * 16 + e * 2 + k)
            put2(4 * d + 2 + k, send2.at[NZ + e], recv_r, r2r, k * 16 + e * 2 + xh)

    put2(0, send2.at[z], recv_l, r2l, r + 1 - 2 * core)
    put2(1, send2.at[NZ + z], recv_r, r2r, (1 - xh) * 16 + z * 2 + xh)
    recv_l[zc] = send2[z]

    @pl.when(core != xh)
    def _():
        put2(2, send2.at[NZ + z], recv_r, r2r, r + 1 - 2 * core)

    @pl.when(core == xh)
    def _():
        recv_r[zc] = send2[NZ + z]

    @pl.loop(0, 16)
    def _(m):
        @pl.when(m != zc)
        def _():
            pltpu.make_async_copy(recv_l.at[m], recv_l.at[m], r2l.at[m]).wait()

        @pl.when(jnp.logical_or(m != zc, core != xh))
        def _():
            pltpu.make_async_copy(recv_r.at[m], recv_r.at[m], r2r.at[m]).wait()

    tri = lax.dot_general(
        recv_l[...].reshape(256, N), recv_r[...].reshape(256, N), (((1,), (1,)), ((), ())), preferred_element_type=F32
    )
    send3[...] = tri.astype(BF16).reshape(16, IL, 256)

    @pl.loop(1, 16)
    def _(d):
        to = (zc + d) % 16
        pltpu.make_async_remote_copy(
            send3.at[to], recv3.at[zc], s3.at[d], r3.at[zc], (xh * 16 + to, c), MESH
        ).start()

    recv3[zc] = send3[zc]

    @pl.loop(1, 16)
    def _(d):
        m = (zc + d) % 16
        pltpu.make_async_copy(recv3.at[m], recv3.at[m], r3.at[m]).wait()

    for a in range(2):
        wide3[256 * a : 256 * a + 256, :] = recv3[:, :, 128 * a : 128 * a + 128].astype(F32).reshape(256, 128)
    for half in range(2):
        for a in range(2):
            for b in range(2):
                parts = []
                for il_half in range(2):
                    tiles = []
                    for q in range(4):
                        il = il_half * 8 + b * 4 + q
                        tiles.append(wide3[pl.ds(256 * a + half * 16 + il, 8, stride=32), :])
                    parts.append(swap_blocks(tiles))
                for q in range(4):
                    send4[half * 8 + a * 4 + q, :, 128 * b : 128 * b + 128] = jnp.concatenate(
                        [parts[0][q], parts[1][q]], axis=0
                    ).astype(BF16)

    @pl.loop(1, COLS)
    def _(d):
        g = (c + d) % COLS
        pltpu.make_async_remote_copy(send4.at[g], recv4.at[c], s4.at[d], r4.at[c], (r, g), MESH).start()

    recv4[c] = send4[c]

    @pl.loop(1, COLS)
    def _(d):
        g = (c + d) % COLS
        pltpu.make_async_copy(recv4.at[g], recv4.at[g], r4.at[g]).wait()

    got = recv4[...].astype(F32)
    for h in range(2):
        tri_t = got[:, 8 * h : 8 * h + 8, :].reshape(C, 256)
        tnorm = layer_norm(tri_t, 0).astype(BF16)
        prod = lax.dot_general(tnorm, ow_ref[...], (((0,), (0,)), ((), ())), preferred_element_type=F32)
        update = gate[256 * h : 256 * h + 256, :] * prod
        out_ref[8 * h : 8 * h + 8] = update.astype(BF16).reshape(8, KL, C)

    @pl.loop(1, COLS)
    def _(d):
        g = (c + d) % COLS
        pltpu.make_async_copy(send1.at[g], send1.at[g], s1.at[d]).wait()
        pltpu.make_async_copy(send4.at[g], send4.at[g], s4.at[d]).wait()
        pltpu.make_async_copy(send3.at[d], send3.at[d], s3.at[d]).wait()

    @pl.loop(4, 32)
    def _(n):
        pltpu.make_async_copy(send2.at[0], send2.at[0], s2.at[n]).wait()

    for n in range(2):
        pltpu.make_async_copy(send2.at[0], send2.at[0], s2.at[n]).wait()

    @pl.when(core != xh)
    def _():
        pltpu.make_async_copy(send2.at[0], send2.at[0], s2.at[2]).wait()


def body(pair, pair_mask, in_weights, gate_weight, out_weight):
    dma = pltpu.SemaphoreType.DMA
    vmem = pltpu.VMEM
    return pl.pallas_call(
        kernel,
        out_shape=jax.ShapeDtypeStruct((IL, KL, C), BF16),
        in_specs=[pl.BlockSpec(memory_space=pl.ANY)] * 5,
        out_specs=pl.BlockSpec(memory_space=vmem),
        scratch_shapes=[
            vmem((IL, KL, C), BF16),
            vmem((IL, KL), jnp.int32),
            vmem((C, 4 * C), BF16),
            vmem((C, C), BF16),
            vmem((C, C), BF16),
            vmem((4 * C, POS), F32),
            vmem((POS, C), F32),
            vmem((COLS, 16, POS), BF16),
            vmem((COLS, 16, POS), BF16),
            vmem((4 * 256, 128), F32),
            vmem((16, IL, N), BF16),
            vmem((16, IL, N), BF16),
            vmem((16, IL, N), BF16),
            vmem((16, IL, 256), BF16),
            vmem((16, IL, 256), BF16),
            vmem((2 * 256, 128), F32),
            vmem((COLS, 16, 256), BF16),
            vmem((COLS, 16, 256), BF16),
            dma((5,)),
            dma((16,)),
            dma((16,)),
            dma((32,)),
            dma((16,)),
            dma((16,)),
            dma((16,)),
            dma((16,)),
            dma((16,)),
            dma((16,)),
        ],
        compiler_params=pltpu.CompilerParams(
            collective_id=0, has_side_effects=True, vmem_limit_bytes=32 * 1024 * 1024
        ),
        cost_estimate=pl.CostEstimate(flops=170_000_000, bytes_accessed=500_000, transcendentals=200_000),
    )(pair, pair_mask, in_weights, gate_weight, out_weight)


def solution(mesh):
    in_specs = (P("row", "col", None), P("row", "col"), P(), P(), P())
    out_specs = P("row", "col", None)
    return jax.shard_map(body, mesh=mesh, in_specs=in_specs, out_specs=out_specs, check_vma=False)
```

time: 463 us -> 58.7 us (0.13)
  waiting for transfers between devices: 427 us -> 0 us
  Pallas kernels: 0 us -> 53.7 us
  between operations: 13.2 us -> 0.01 us
  other arithmetic: 6.94 us -> 0 us
  local copies, waits for them, and re-layouts: 10.8 us -> 4.68 us
  matrix products: 4.75 us -> 0 us
    psum x1 -> x0, waiting for transfers between devices: 291 us -> none  [spread(): return lax.psum(jnp.where(mine, value, jnp.zeros_like(value)), axis)]
    all_gather x2 -> x0, waiting for transfers between devices: 136 us -> none  [the longest x1 69.3 us: body(): lax.all_gather(right, 'col', axis=1, tiled=True)]
    pallas_call x0 -> x1, Pallas kernels: none -> 53.7 us  [body(): pl.pallas_call(kernel, out_shape=jax.ShapeDtypeStruct((IL, KL, C), BF16),...]
    all_gather x2 -> x0, local copies, waits for them, and re-layouts: 7.83 us -> none  [the longest x1 3.92 us: body(): lax.all_gather(right, 'col', axis=1, tiled=True)]
    dot_general x4 -> x0, matrix products: 4.75 us -> none  [the longest x1 3.43 us: body(): jnp.einsum('ikc,jkc->ijc', left_rows, partner, preferred_element_type=jnp...]
  transfers between devices with their start and end apart: 3 -> 0, of which waited for: 3 -> 0; matrix products, arithmetic and copies ran while one was open for 2% -> 0% of each run, Pallas kernels for 0% -> 0%
where the time goes in v1:
time: 58.7 us; the launch traced here: 58.4 us
  Pallas kernels  53.7 us (91%)
  local copies, waits for them, and re-layouts  4.68 us (8%)
    pallas_call x1, Pallas kernels, body(): pl.pallas_call(kernel, out_shape=jax.ShapeDtypeStruct((IL, KL, C), BF16),...  53.7 us
    unnamed x11, local copies, waits for them, and re-layouts  4.68 us

profile of v1, /device:TPU:1, one launch (start us, length us, event | category | flops | bytes accessed | tf_op | source)
XLA Modules:
  0.0 58.4 jit_solution(7734670317454946923)
XLA Ops:
  0.0 0.0 copy-start
  0.0 0.9 %copy-done = bf16[16,32,128]{2,1,0:T(8,128)(2,1)S(1)} copy-done((bf16[16,32,128]{2,1,0:T(8,128)(2,1)S(1)}, bf16[16,32,128]{2,1,0:T(8,128)(2,1)}, u32[]{:S(2)}) %copy-start) | copy-done | bytes 131096
  0.9 0.0 copy-start.1
  0.9 0.9 %copy-done.1 = bf16[128,512]{1,0:T(8,128)(2,1)S(1)} copy-done((bf16[128,512]{1,0:T(8,128)(2,1)S(1)}, bf16[128,512]{1,0:T(8,128)(2,1)}, u32[]{:S(2)}) %copy-start.1) | copy-done | bytes 131096
  1.8 0.0 copy-start.2
  1.8 0.8 %copy-done.2 = bf16[128,128]{1,0:T(8,128)(2,1)S(1)} copy-done((bf16[128,128]{1,0:T(8,128)(2,1)S(1)}, bf16[128,128]{1,0:T(8,128)(2,1)}, u32[]{:S(2)}) %copy-start.2) | copy-done | bytes 32792
  2.6 0.0 copy-start.3
  2.6 0.8 %copy-done.3 = bf16[128,128]{1,0:T(8,128)(2,1)S(1)} copy-done((bf16[128,128]{1,0:T(8,128)(2,1)S(1)}, bf16[128,128]{1,0:T(8,128)(2,1)}, u32[]{:S(2)}) %copy-start.3) | copy-done | bytes 32792
  3.3 0.0 copy-start.4
  3.3 0.7 %copy-done.4 = s32[16,32]{1,0:T(8,128)S(1)} copy-done((s32[16,32]{1,0:T(8,128)S(1)}, s32[16,32]{1,0:T(8,128)}, u32[]{:S(2)}) %copy-start.4) | copy-done | bytes 2072
  4.0 53.7 %shard_map.55 = bf16[16,32,128]{2,1,0:T(8,128)(2,1)S(1)} custom-call(bf16[16,32,128]{2,1,0:T(8,128)(2,1)S(1)} %copy-done, s32[16,32]{1,0:T(8,128)S(1)} %copy-done.4, bf16[128,512]{1,0:T(8,128)(2,1)S(1)} %copy-done.1, bf16[128,128]{1,0:T(8,128)(2,1)S(1)} %copy-done.2, bf16[128,128]{1,0:T(8,128)(2,1)S(1)} %copy-done.3), custom_call_target="tpu_custom_call" | custom-call | flops 170000000 | bytes 500000 | tf_op jit(solution)/shard_map/pallas_call | solution.py:228
  57.7 0.7 %copy.7 = bf16[16,32,128]{2,1,0:T(8,128)(2,1)} copy(bf16[16,32,128]{2,1,0:T(8,128)(2,1)S(1)} %shard_map.55) | data formatting | bytes 262144
Async XLA Ops:
  0.0 0.9 %copy-start = (bf16[16,32,128]{2,1,0:T(8,128)(2,1)S(1)}, bf16[16,32,128]{2,1,0:T(8,128)(2,1)}, u32[]{:S(2)}) copy-start(bf16[16,32,128]{2,1,0:T(8,128)(2,1)} %pair_hbm.1) | copy-start | bytes 393220
  0.9 0.9 %copy-start.1 = (bf16[128,512]{1,0:T(8,128)(2,1)S(1)}, bf16[128,512]{1,0:T(8,128)(2,1)}, u32[]{:S(2)}) copy-start(bf16[128,512]{1,0:T(8,128)(2,1)} %w_hbm.1) | copy-start | bytes 393220
  1.8 0.8 %copy-start.2 = (bf16[128,128]{1,0:T(8,128)(2,1)S(1)}, bf16[128,128]{1,0:T(8,128)(2,1)}, u32[]{:S(2)}) copy-start(bf16[128,128]{1,0:T(8,128)(2,1)} %gw_hbm.1) | copy-start | bytes 98308
  2.6 0.8 %copy-start.3 = (bf16[128,128]{1,0:T(8,128)(2,1)S(1)}, bf16[128,128]{1,0:T(8,128)(2,1)}, u32[]{:S(2)}) copy-start(bf16[128,128]{1,0:T(8,128)(2,1)} %ow_hbm.1) | copy-start | bytes 98308
  3.3 0.7 %copy-start.4 = (s32[16,32]{1,0:T(8,128)S(1)}, s32[16,32]{1,0:T(8,128)}, u32[]{:S(2)}) copy-start(s32[16,32]{1,0:T(8,128)} %mask_hbm.1) | copy-start | bytes 6148

commit v2 on v0

v2 whole, which is shorter than its diff:
```python
import jax
import jax.numpy as jnp
from jax import lax
from jax.experimental import pallas as pl
from jax.experimental.pallas import tpu as pltpu
from jax.sharding import PartitionSpec as P

MESH = pl.DeviceIdType.MESH
F32 = jnp.float32
BF16 = jnp.bfloat16

ROWS, COLS = 32, 16
NZ = 8
IL, KL = 16, 32
N = 512
POS = IL * KL
C = 128


def layer_norm(values, axis):
    mean = jnp.mean(values, axis=axis, keepdims=True)
    centred = values - mean
    var = jnp.mean(centred * centred, axis=axis, keepdims=True)
    return centred * lax.rsqrt(var + 1e-05)


def sigmoid(x):
    return 0.5 * jnp.tanh(0.5 * x) + 0.5


def swap_blocks(v):
    v = list(v)
    lane = lax.broadcasted_iota(jnp.int32, v[0].shape, 1)
    apart, width = len(v) // 2, 64
    while apart:
        low = (lane % (2 * width)) < width
        for n in range(len(v)):
            if n % (2 * apart) < apart:
                x, y = v[n], v[n + apart]
                v[n] = jnp.where(low, x, pltpu.roll(y, width, 1))
                v[n + apart] = jnp.where(low, pltpu.roll(x, 128 - width, 1), y)
        apart, width = apart // 2, width // 2
    return v


def landed(ref, sem):
    pltpu.make_async_copy(ref, ref, sem).wait()


def kernel(
    pair_hbm, mask_hbm, w_hbm, gw_hbm, ow_hbm, out_ref,
    pair_ref, mask_ref, w_ref, gw_ref, ow_ref, proj, gate,
    send_l1, recv_l1, send_r1, recv_r1, turn_l, turn_r, send_l2, recv_l2, send_r2, recv_r2, turn_r2, right,
    tri_ref, send_a3, recv_a3, wide_a, send_a4, recv_a4, send_b3, recv_b3, wide_b, send_b4, recv_b4, ow_wide, ow_turned,
    load_sem, sl1, rl1, sr1, rr1, sl2, rl2, sr2, rr2, s3a, r3a, s4a, r4a, s3b, r3b, s4b, r4b,
):
    r, c = lax.axis_index("row"), lax.axis_index("col")
    xh, z, core = r // 16, (r // 2) % NZ, r % 2
    zc = r % 16

    def far(n):
        return 4 + (1 - 2 * (n % 2)) * ((n + 1) // 2)

    def col_peer(n):
        return (c // 8 + 1 - n % 2) % 2 * 8 + (c + far(n // 2)) % 8

    def zc_peer(n):
        return (z + far(n // 2)) % NZ * 2 + (core + 1 - n % 2) % 2

    def row(xh, z, core):
        return xh * 16 + z * 2 + core

    def send(src, dst, ssem, rsem, to_row, to_col):
        pltpu.make_async_remote_copy(src, dst, ssem, rsem, (to_row, to_col), MESH).start()

    loads = []
    for n, (src, dst) in enumerate(
        ((pair_hbm, pair_ref), (mask_hbm, mask_ref), (w_hbm, w_ref), (gw_hbm, gw_ref), (ow_hbm, ow_ref))
    ):
        loads.append(pltpu.make_async_copy(src, dst, load_sem.at[n]))
        loads[-1].start()

    barrier = pltpu.get_barrier_semaphore()

    def greet(to_row, to_col):
        pl.semaphore_signal(barrier, inc=1, device_id=(to_row, to_col), device_id_type=MESH)

    @pl.loop(1, COLS)
    def _(d):
        greet(r, (c + d) % COLS)

    @pl.loop(0, COLS)
    def _(d):
        greet((r + 16) % ROWS, (c + d) % COLS)

    @pl.loop(1, 16)
    def _(d):
        greet(xh * 16 + (zc + d) % 16, c)

    for load in loads:
        load.wait()

    normed = layer_norm(pair_ref[...].reshape(POS, C).astype(F32), 1)
    eye = lax.broadcasted_iota(jnp.int32, (KL, KL), 0) == lax.broadcasted_iota(jnp.int32, (KL, KL), 1)
    maskf = mask_ref[...].astype(F32)
    column = jnp.concatenate(
        [jnp.sum(jnp.where(eye, maskf[il : il + 1, :], 0.0), axis=1, keepdims=True) for il in range(IL)], axis=0
    )
    masked = (normed * column).astype(BF16)
    normed = normed.astype(BF16)
    full = lax.dot_general(w_ref[...], masked, (((0,), (1,)), ((), ())), preferred_element_type=F32)
    for t in range(4):
        proj[512 * t : 512 * t + 512, :] = full[:, 128 * t : 128 * t + 128]

    pl.semaphore_wait(barrier, 46)

    def left_of(g):
        x = []
        for t in range(4):
            at = [pl.ds(pl.multiple_of(512 * t + block * C + g * 8, 8), 8) for block in range(2)]
            x.append(sigmoid(proj[at[1], :]) * proj[at[0], :])
        x = [jnp.concatenate([x[n], x[n + 2]], axis=0) for n in range(2)]
        return jnp.concatenate(x, axis=1).astype(BF16)

    def right_of(e):
        x = []
        for t in range(4):
            at = [pl.ds(512 * t + block * C + e, 16, stride=8) for block in (2, 3)]
            x.append(sigmoid(proj[at[1], :]) * proj[at[0], :])
        return jnp.concatenate(x, axis=1).astype(BF16)

    def put_left1(n):
        g = col_peer(n)
        send_l1[g] = left_of(g)
        send(send_l1.at[g], recv_l1.at[c], sl1.at[g], rl1.at[c], r, g)

    @pl.loop(0, 7)
    def _(n):
        e = (z + far(n)) % NZ
        send_r1[e] = right_of(e)
        send(send_r1.at[e], recv_r1.at[z], sr1.at[e], rr1.at[z], row(xh, e, core), c)
        put_left1(2 * n)
        put_left1(2 * n + 1)

    put_left1(14)
    recv_r1[z] = right_of(z)
    recv_l1[c] = left_of(c)
    @pl.loop(0, 7)
    def _(n):
        e = (z + far(n)) % NZ
        landed(recv_r1.at[e], rr1.at[e])

    for t in range(4):
        turn_r[128 * t : 128 * t + 128, :] = recv_r1[:, :, 128 * t : 128 * t + 128].astype(F32).reshape(128, 128)
    for g in range(COLS):
        x = [turn_r[pl.ds(128 * t + g, 8, stride=16), :] for t in range(4)]
        for n in range(2):
            send_r2[g, :, 128 * n : 128 * n + 128] = jnp.concatenate([x[n], x[n + 2]], axis=0).astype(BF16)

    @pl.loop(0, 31)
    def _(n):
        g, to = col_peer(n // 2), (xh + 1 - n % 2) % 2
        send(send_r2.at[g], recv_r2.at[xh * 16 + c], sr2.at[n], rr2.at[xh * 16 + c], row(to, z, core), g)

    recv_r2[xh * 16 + c] = send_r2[c]

    @pl.loop(0, 15)
    def _(n):
        g = col_peer(n)
        landed(recv_l1.at[g], rl1.at[g])

    for a in range(4):
        for b in range(2):
            tiles = [recv_l1[4 * a + q, :, 128 * b : 128 * b + 128].astype(F32) for q in range(4)]
            for q, tile in enumerate(swap_blocks(tiles)):
                at = 128 * a + 16 * (4 * b + q)
                turn_l[at : at + 16, :] = tile
    for e in range(NZ):
        for a in range(4):
            x = [turn_l[pl.ds(128 * a + 8 * h + e, 8, stride=16), :] for h in range(2)]
            send_l2[e, :, 128 * a : 128 * a + 128] = jnp.concatenate(x, axis=0).astype(BF16)

    @pl.loop(0, 15)
    def _(n):
        to = zc_peer(n)
        send(send_l2.at[to // 2], recv_l2.at[zc], sl2.at[to], rl2.at[zc], xh * 16 + to, c)

    recv_l2[zc] = send_l2[z]

    ow_wide[...] = ow_ref[...].astype(F32)
    for e in range(NZ):
        ow_turned[16 * e : 16 * e + 16, :] = ow_wide[pl.ds(e, 16, stride=8), :].astype(BF16)
    gate[...] = sigmoid(jnp.dot(normed, gw_ref[...], preferred_element_type=F32)).reshape(IL, KL, C)

    @pl.loop(1, 32)
    def _(d):
        m = (xh * 16 + c + d) % 32
        landed(recv_r2.at[m], rr2.at[m])

    for h in range(2):
        for a in range(4):
            for b in range(2):
                tiles = [recv_r2[16 * h + 4 * a + q, :, 128 * b : 128 * b + 128].astype(F32) for q in range(4)]
                for q, tile in enumerate(swap_blocks(tiles)):
                    at = 256 * a + 128 * h + 16 * (4 * b + q)
                    turn_r2[at : at + 16, :] = tile
        for m in range(NZ):
            for a in range(4):
                x = [turn_r2[pl.ds(256 * a + 128 * h + 8 * jh + m, 8, stride=16), :] for jh in range(2)]
                at = 128 * h + 16 * m
                right[at : at + 16, 128 * a : 128 * a + 128] = jnp.concatenate(x, axis=0).astype(BF16)

    @pl.loop(0, 15)
    def _(n):
        m = zc_peer(n)
        landed(recv_l2.at[m], rl2.at[m])

    tri = lax.dot_general(
        recv_l2[...].reshape(256, N), right[...], (((1,), (1,)), ((), ())), preferred_element_type=F32
    )
    upper = tri.reshape(16, 2, 8, 256)[:, 0]
    send_a3[...] = jnp.concatenate([upper[:, :, :128], upper[:, :, 128:]], axis=1).astype(BF16)

    @pl.loop(0, 15)
    def _(n):
        to = zc_peer(n)
        send(send_a3.at[to], recv_a3.at[zc], s3a.at[to], r3a.at[zc], xh * 16 + to, c)

    for a in range(2):
        tri_ref[256 * a : 256 * a + 256, :] = tri[:, 128 * a : 128 * a + 128]
    for a in range(2):
        tiles = [tri_ref[pl.ds(256 * a + 8 + q, 16, stride=16), :] for q in range(8)]
        for q, tile in enumerate(swap_blocks(tiles)):
            send_b3[8 * a + q] = tile.astype(BF16)

    @pl.loop(0, 15)
    def _(n):
        g = col_peer(n)
        send(send_b3.at[g], recv_b3.at[c], s3b.at[g], r3b.at[c], r, g)

    recv_a3[zc] = send_a3[zc]
    recv_b3[c] = send_b3[c]

    @pl.loop(0, 15)
    def _(n):
        m = zc_peer(n)
        landed(recv_a3.at[m], r3a.at[m])

    wide_a[...] = recv_a3[...].astype(F32).reshape(256, 128)
    for a in range(2):
        parts = []
        for k in range(2):
            parts.append(swap_blocks([wide_a[pl.ds(16 * k + 8 * a + q, 8, stride=32), :] for q in range(8)]))
        for q in range(8):
            send_a4[8 * a + q] = jnp.concatenate([parts[0][q], parts[1][q]], axis=0).astype(BF16)

    @pl.loop(0, 15)
    def _(n):
        g = col_peer(n)
        send(send_a4.at[g], recv_a4.at[c], s4a.at[g], r4a.at[c], r, g)

    @pl.loop(0, 15)
    def _(n):
        g = col_peer(n)
        landed(recv_b3.at[g], r3b.at[g])

    wide_b[...] = recv_b3[...].astype(F32).reshape(256, 128)
    for m in range(16):
        send_b4[m] = wide_b[pl.ds(m, 16, stride=16), :].astype(BF16)

    @pl.loop(0, 15)
    def _(n):
        to = zc_peer(n)
        send(send_b4.at[to], recv_b4.at[zc], s4b.at[to], r4b.at[zc], xh * 16 + to, c)

    recv_a4[c] = send_a4[c]
    recv_b4[zc] = send_b4[zc]

    def finish(tri_t, k, h, weight):
        tnorm = layer_norm(tri_t, 0).astype(BF16)
        prod = lax.dot_general(tnorm, weight, (((0,), (0,)), ((), ())), preferred_element_type=F32)
        update = gate[8 * h : 8 * h + 8, 16 * k : 16 * k + 16, :] * prod.reshape(8, 16, C)
        out_ref[8 * h : 8 * h + 8, 16 * k : 16 * k + 16, :] = update.astype(BF16)

    @pl.loop(0, 15)
    def _(n):
        g = col_peer(n)
        landed(recv_a4.at[g], r4a.at[g])

    got = recv_a4[...].astype(F32)
    for k in range(2):
        finish(got[:, 8 * k : 8 * k + 8, :].reshape(C, 128), k, 0, ow_ref[...])

    @pl.loop(0, 15)
    def _(n):
        m = zc_peer(n)
        landed(recv_b4.at[m], r4b.at[m])

    got = recv_b4[...].astype(F32).reshape(NZ, 2, 16, 128)
    for k in range(2):
        finish(got[:, k].reshape(C, 128), k, 1, ow_turned[...])

    @pl.loop(0, 15)
    def _(n):
        g, m = col_peer(n), zc_peer(n)
        landed(send_l1.at[g], sl1.at[g])
        landed(send_l2.at[0], sl2.at[m])
        landed(send_a3.at[m], s3a.at[m])
        landed(send_b3.at[g], s3b.at[g])
        landed(send_a4.at[g], s4a.at[g])
        landed(send_b4.at[m], s4b.at[m])

    @pl.loop(0, 7)
    def _(n):
        e = (z + far(n)) % NZ
        landed(send_r1.at[e], sr1.at[e])

    @pl.loop(0, 31)
    def _(n):
        landed(send_r2.at[0], sr2.at[n])


def body(pair, pair_mask, in_weights, gate_weight, out_weight):
    dma = pltpu.SemaphoreType.DMA
    vmem = pltpu.VMEM
    return pl.pallas_call(
        kernel,
        out_shape=jax.ShapeDtypeStruct((IL, KL, C), BF16),
        in_specs=[pl.BlockSpec(memory_space=pl.ANY)] * 5,
        out_specs=pl.BlockSpec(memory_space=vmem),
        scratch_shapes=[
            vmem((IL, KL, C), BF16),
            vmem((IL, KL), jnp.int32),
            vmem((C, 4 * C), BF16),
            vmem((C, C), BF16),
            vmem((C, C), BF16),
            vmem((4 * 512, 128), F32),
            vmem((IL, KL, C), F32),
            vmem((COLS, 16, 256), BF16),
            vmem((COLS, 16, 256), BF16),
            vmem((NZ, 16, POS), BF16),
            vmem((NZ, 16, POS), BF16),
            vmem((4 * 128, 128), F32),
            vmem((4 * 128, 128), F32),
            vmem((NZ, 16, N), BF16),
            vmem((16, 16, N), BF16),
            vmem((COLS, 16, 256), BF16),
            vmem((2 * COLS, 16, 256), BF16),
            vmem((4 * 256, 128), F32),
            vmem((256, N), BF16),
            vmem((2 * 256, 128), F32),
            vmem((16, 16, 128), BF16),
            vmem((16, 16, 128), BF16),
            vmem((256, 128), F32),
            vmem((16, 16, 128), BF16),
            vmem((16, 16, 128), BF16),
            vmem((16, 16, 128), BF16),
            vmem((16, 16, 128), BF16),
            vmem((256, 128), F32),
            vmem((16, 16, 128), BF16),
            vmem((16, 16, 128), BF16),
            vmem((C, C), F32),
            vmem((C, C), BF16),
            dma((5,)),
            dma((16,)),
            dma((16,)),
            dma((8,)),
            dma((8,)),
            dma((16,)),
            dma((16,)),
            dma((32,)),
            dma((32,)),
            dma((16,)),
            dma((16,)),
            dma((16,)),
            dma((16,)),
            dma((16,)),
            dma((16,)),
            dma((16,)),
            dma((16,)),
        ],
        compiler_params=pltpu.CompilerParams(
            collective_id=0, has_side_effects=True, vmem_limit_bytes=58 * 1024 * 1024
        ),
        cost_estimate=pl.CostEstimate(flops=170_000_000, bytes_accessed=500_000, transcendentals=200_000),
    )(pair, pair_mask, in_weights, gate_weight, out_weight)


def solution(mesh):
    in_specs = (P("row", "col", None), P("row", "col"), P(), P(), P())
    out_specs = P("row", "col", None)
    return jax.shard_map(body, mesh=mesh, in_specs=in_specs, out_specs=out_specs, check_vma=False)
```

time: 463 us -> 48.3 us (0.10)
  waiting for transfers between devices: 427 us -> 0 us
  Pallas kernels: 0 us -> 46.6 us
  between operations: 13.2 us -> 0.01 us
  local copies, waits for them, and re-layouts: 10.8 us -> 1.57 us
  other arithmetic: 6.94 us -> 0 us
  matrix products: 4.75 us -> 0 us
    psum x1 -> x0, waiting for transfers between devices: 291 us -> none  [spread(): return lax.psum(jnp.where(mine, value, jnp.zeros_like(value)), axis)]
    all_gather x2 -> x0, waiting for transfers between devices: 136 us -> none  [the longest x1 69.3 us: body(): lax.all_gather(right, 'col', axis=1, tiled=True)]
    pallas_call x0 -> x1, Pallas kernels: none -> 46.6 us  [body(): pl.pallas_call(kernel, out_shape=jax.ShapeDtypeStruct((IL, KL, C), BF16),...]
    all_gather x2 -> x0, local copies, waits for them, and re-layouts: 7.83 us -> none  [the longest x1 3.92 us: body(): lax.all_gather(right, 'col', axis=1, tiled=True)]
    dot_general x4 -> x0, matrix products: 4.75 us -> none  [the longest x1 3.43 us: body(): jnp.einsum('ikc,jkc->ijc', left_rows, partner, preferred_element_type=jnp...]
  transfers between devices with their start and end apart: 3 -> 0, of which waited for: 3 -> 0; matrix products, arithmetic and copies ran while one was open for 2% -> 0% of each run, Pallas kernels for 0% -> 0%
where the time goes in v2:
time: 48.3 us; the launch traced here: 48.2 us
  Pallas kernels  46.6 us (96%)
  local copies, waits for them, and re-layouts  1.57 us (3%)
    pallas_call x1, Pallas kernels, body(): pl.pallas_call(kernel, out_shape=jax.ShapeDtypeStruct((IL, KL, C), BF16),...  46.6 us
    unnamed x1, local copies, waits for them, and re-layouts  1.57 us

profile of v2, /device:TPU:1, one launch (start us, length us, event | category | flops | bytes accessed | tf_op | source)
XLA Modules:
  0.0 48.2 jit_solution(11542351642137648963)
XLA Ops:
  0.0 46.6 %shard_map.55 = bf16[16,32,128]{2,1,0:T(8,128)(2,1)} custom-call(bf16[16,32,128]{2,1,0:T(8,128)(2,1)} %pair_hbm.1, s32[16,32]{1,0:T(8,128)} %mask_hbm.1, bf16[128,512]{1,0:T(8,128)(2,1)} %w_hbm.1, bf16[128,128]{1,0:T(8,128)(2,1)} %gw_hbm.1, bf16[128,128]{1,0:T(8,128)(2,1)} %ow_hbm.1), custom_call_target="tpu_custom_call" | custom-call | flops 170000000 | bytes 500000 | tf_op jit(solution)/shard_map/pallas_call | solution.py:326
  46.6 1.6 %copy.7 = bf16[16,32,128]{2,1,0:T(8,128)(2,1)} copy(bf16[16,32,128]{2,1,0:T(8,128)(2,1)} %shard_map.55) | data formatting | bytes 262144

commit v3 on v2

--- a/solution.py
+++ b/solution.py
@@ -51,8 +51,8 @@
     pair_hbm, mask_hbm, w_hbm, gw_hbm, ow_hbm, out_ref,
     pair_ref, mask_ref, w_ref, gw_ref, ow_ref, proj, gate,
     send_l1, recv_l1, send_r1, recv_r1, turn_l, turn_r, send_l2, recv_l2, send_r2, recv_r2, turn_r2, right,
-    tri_ref, send_a3, recv_a3, wide_a, send_a4, recv_a4, send_b3, recv_b3, wide_b, send_b4, recv_b4, ow_wide, ow_turned,
-    load_sem, sl1, rl1, sr1, rr1, sl2, rl2, sr2, rr2, s3a, r3a, s4a, r4a, s3b, r3b, s4b, r4b,
+    send3, recv3, wide3, send4, recv4,
+    met, load_sem, sl1, rl1, sr1, rr1, sl2, rl2, sr2, rr2, s3, r3, s4, r4,
 ):
     r, c = lax.axis_index("row"), lax.axis_index("col")
     xh, z, core = r // 16, (r // 2) % NZ, r % 2
@@ -85,19 +85,20 @@
     def greet(to_row, to_col):
         pl.semaphore_signal(barrier, inc=1, device_id=(to_row, to_col), device_id_type=MESH)
 
+    sibling, partner = r + 1 - 2 * core, (r + 16) % ROWS
+
     @pl.loop(1, COLS)
     def _(d):
         greet(r, (c + d) % COLS)
 
-    @pl.loop(0, COLS)
+    @pl.loop(1, NZ)
     def _(d):
-        greet((r + 16) % ROWS, (c + d) % COLS)
-
-    @pl.loop(1, 16)
-    def _(d):
-        greet(xh * 16 + (zc + d) % 16, c)
-
-    for load in loads:
+        greet(row(xh, (z + d) % NZ, core), c)
+
+    greet(sibling, c)
+    greet(partner, c)
+
+    for load in loads[:2]:
         load.wait()
 
     normed = layer_norm(pair_ref[...].reshape(POS, C).astype(F32), 1)
@@ -108,11 +109,14 @@
     )
     masked = (normed * column).astype(BF16)
     normed = normed.astype(BF16)
+    loads[2].wait()
     full = lax.dot_general(w_ref[...], masked, (((0,), (1,)), ((), ())), preferred_element_type=F32)
     for t in range(4):
         proj[512 * t : 512 * t + 512, :] = full[:, 128 * t : 128 * t + 128]
 
-    pl.semaphore_wait(barrier, 46)
+    pl.semaphore_wait(barrier, 24)
+    for to in (sibling, partner):
+        pl.semaphore_signal(met, inc=1, device_id=(to, c), device_id_type=MESH)
 
     def left_of(g):
         x = []
@@ -156,6 +160,8 @@
         x = [turn_r[pl.ds(128 * t + g, 8, stride=16), :] for t in range(4)]
         for n in range(2):
             send_r2[g, :, 128 * n : 128 * n + 128] = jnp.concatenate([x[n], x[n + 2]], axis=0).astype(BF16)
+
+    pl.semaphore_wait(met, 2)
 
     @pl.loop(0, 31)
     def _(n):
@@ -180,16 +186,32 @@
             x = [turn_l[pl.ds(128 * a + 8 * h + e, 8, stride=16), :] for h in range(2)]
             send_l2[e, :, 128 * a : 128 * a + 128] = jnp.concatenate(x, axis=0).astype(BF16)
 
-    @pl.loop(0, 15)
-    def _(n):
-        to = zc_peer(n)
-        send(send_l2.at[to // 2], recv_l2.at[zc], sl2.at[to], rl2.at[zc], xh * 16 + to, c)
+    @pl.loop(0, 7)
+    def _(n):
+        e = (z + far(n)) % NZ
+        send(send_l2.at[e], recv_l2.at[zc], sl2.at[n], rl2.at[zc], row(xh, e, core), c)
 
     recv_l2[zc] = send_l2[z]
-
-    ow_wide[...] = ow_ref[...].astype(F32)
-    for e in range(NZ):
-        ow_turned[16 * e : 16 * e + 16, :] = ow_wide[pl.ds(e, 16, stride=8), :].astype(BF16)
+    send(send_l2.at[z], recv_l2.at[zc], sl2.at[7], rl2.at[zc], sibling, c)
+
+    def pass_right(i):
+        m = xh * 16 + col_peer(14 - i)
+        landed(recv_r2.at[m], rr2.at[m])
+        send(recv_r2.at[m], recv_r2.at[m], sr2.at[18 + i], rr2.at[m], partner, c)
+
+    def pass_left(i):
+        m = (z + far(6 - i)) % NZ * 2 + core
+        landed(recv_l2.at[m], rl2.at[m])
+        send(recv_l2.at[m], recv_l2.at[m], sl2.at[8 + i], rl2.at[m], sibling, c)
+
+    @pl.loop(0, 6)
+    def _(i):
+        pass_left(i)
+
+    pass_left(6)
+
+    loads[3].wait()
+    loads[4].wait()
     gate[...] = sigmoid(jnp.dot(normed, gw_ref[...], preferred_element_type=F32)).reshape(IL, KL, C)
 
     @pl.loop(1, 32)
@@ -210,105 +232,69 @@
                 at = 128 * h + 16 * m
                 right[at : at + 16, 128 * a : 128 * a + 128] = jnp.concatenate(x, axis=0).astype(BF16)
 
-    @pl.loop(0, 15)
-    def _(n):
-        m = zc_peer(n)
+    @pl.loop(0, NZ)
+    def _(e):
+        m = 2 * e + 1 - core
         landed(recv_l2.at[m], rl2.at[m])
 
     tri = lax.dot_general(
         recv_l2[...].reshape(256, N), right[...], (((1,), (1,)), ((), ())), preferred_element_type=F32
     )
-    upper = tri.reshape(16, 2, 8, 256)[:, 0]
-    send_a3[...] = jnp.concatenate([upper[:, :, :128], upper[:, :, 128:]], axis=1).astype(BF16)
+    send3[...] = tri.astype(BF16).reshape(16, IL, 256)
 
     @pl.loop(0, 15)
     def _(n):
         to = zc_peer(n)
-        send(send_a3.at[to], recv_a3.at[zc], s3a.at[to], r3a.at[zc], xh * 16 + to, c)
+        send(send3.at[to], recv3.at[zc], s3.at[to], r3.at[zc], xh * 16 + to, c)
+
+    recv3[zc] = send3[zc]
+
+    @pl.loop(0, 15)
+    def _(n):
+        m = zc_peer(n)
+        landed(recv3.at[m], r3.at[m])
 
     for a in range(2):
-        tri_ref[256 * a : 256 * a + 256, :] = tri[:, 128 * a : 128 * a + 128]
+        wide3[256 * a : 256 * a + 256, :] = recv3[:, :, 128 * a : 128 * a + 128].astype(F32).reshape(256, 128)
     for a in range(2):
-        tiles = [tri_ref[pl.ds(256 * a + 8 + q, 16, stride=16), :] for q in range(8)]
-        for q, tile in enumerate(swap_blocks(tiles)):
-            send_b3[8 * a + q] = tile.astype(BF16)
+        for k in range(2):
+            parts = []
+            for h in range(2):
+                at = 256 * a + 16 * k + 8 * h
+                parts.append(swap_blocks([wide3[pl.ds(at + q, 8, stride=32), :] for q in range(8)]))
+            for q in range(8):
+                send4[8 * a + q, :, 128 * k : 128 * k + 128] = jnp.concatenate(
+                    [parts[0][q], parts[1][q]], axis=0
+                ).astype(BF16)
 
     @pl.loop(0, 15)
     def _(n):
         g = col_peer(n)
-        send(send_b3.at[g], recv_b3.at[c], s3b.at[g], r3b.at[c], r, g)
-
-    recv_a3[zc] = send_a3[zc]
-    recv_b3[c] = send_b3[c]
-
-    @pl.loop(0, 15)
-    def _(n):
-        m = zc_peer(n)
-        landed(recv_a3.at[m], r3a.at[m])
-
-    wide_a[...] = recv_a3[...].astype(F32).reshape(256, 128)
-    for a in range(2):
-        parts = []
+        send(send4.at[g], recv4.at[c], s4.at[g], r4.at[c], r, g)
+
+    recv4[c] = send4[c]
+
+    @pl.loop(0, 15)
+    def _(n):
+        g = col_peer(n)
+        landed(recv4.at[g], r4.at[g])
+
+    got = recv4[...].astype(F32)
+    for h in range(2):
+        tnorm = layer_norm(got[:, 8 * h : 8 * h + 8, :].reshape(C, 256), 0).astype(BF16)
+        prod = lax.dot_general(tnorm, ow_ref[...], (((0,), (0,)), ((), ())), preferred_element_type=F32)
         for k in range(2):
-            parts.append(swap_blocks([wide_a[pl.ds(16 * k + 8 * a + q, 8, stride=32), :] for q in range(8)]))
-        for q in range(8):
-            send_a4[8 * a + q] = jnp.concatenate([parts[0][q], parts[1][q]], axis=0).astype(BF16)
-
-    @pl.loop(0, 15)
-    def _(n):
-        g = col_peer(n)
-        send(send_a4.at[g], recv_a4.at[c], s4a.at[g], r4a.at[c], r, g)
-
-    @pl.loop(0, 15)
-    def _(n):
-        g = col_peer(n)
-        landed(recv_b3.at[g], r3b.at[g])
-
-    wide_b[...] = recv_b3[...].astype(F32).reshape(256, 128)
-    for m in range(16):
-        send_b4[m] = wide_b[pl.ds(m, 16, stride=16), :].astype(BF16)
-
-    @pl.loop(0, 15)
-    def _(n):
-        to = zc_peer(n)
-        send(send_b4.at[to], recv_b4.at[zc], s4b.at[to], r4b.at[zc], xh * 16 + to, c)
-
-    recv_a4[c] = send_a4[c]
-    recv_b4[zc] = send_b4[zc]
-
-    def finish(tri_t, k, h, weight):
-        tnorm = layer_norm(tri_t, 0).astype(BF16)
-        prod = lax.dot_general(tnorm, weight, (((0,), (0,)), ((), ())), preferred_element_type=F32)
-        update = gate[8 * h : 8 * h + 8, 16 * k : 16 * k + 16, :] * prod.reshape(8, 16, C)
-        out_ref[8 * h : 8 * h + 8, 16 * k : 16 * k + 16, :] = update.astype(BF16)
-
-    @pl.loop(0, 15)
-    def _(n):
-        g = col_peer(n)
-        landed(recv_a4.at[g], r4a.at[g])
-
-    got = recv_a4[...].astype(F32)
-    for k in range(2):
-        finish(got[:, 8 * k : 8 * k + 8, :].reshape(C, 128), k, 0, ow_ref[...])
-
-    @pl.loop(0, 15)
-    def _(n):
-        m = zc_peer(n)
-        landed(recv_b4.at[m], r4b.at[m])
-
-    got = recv_b4[...].astype(F32).reshape(NZ, 2, 16, 128)
-    for k in range(2):
-        finish(got[:, k].reshape(C, 128), k, 1, ow_turned[...])
+            part = prod[128 * k : 128 * k + 128, :].reshape(8, 16, C)
+            update = gate[8 * h : 8 * h + 8, 16 * k : 16 * k + 16, :] * part
+            out_ref[8 * h : 8 * h + 8, 16 * k : 16 * k + 16, :] = update.astype(BF16)
 
     @pl.loop(0, 15)
     def _(n):
         g, m = col_peer(n), zc_peer(n)
         landed(send_l1.at[g], sl1.at[g])
-        landed(send_l2.at[0], sl2.at[m])
-        landed(send_a3.at[m], s3a.at[m])
-        landed(send_b3.at[g], s3b.at[g])
-        landed(send_a4.at[g], s4a.at[g])
-        landed(send_b4.at[m], s4b.at[m])
+        landed(send_l2.at[0], sl2.at[n])
+        landed(send3.at[m], s3.at[m])
+        landed(send4.at[g], s4.at[g])
 
     @pl.loop(0, 7)
     def _(n):
@@ -348,19 +334,12 @@
             vmem((2 * COLS, 16, 256), BF16),
             vmem((4 * 256, 128), F32),
             vmem((256, N), BF16),
+            vmem((16, IL, 256), BF16),
+            vmem((16, IL, 256), BF16),
             vmem((2 * 256, 128), F32),
-            vmem((16, 16, 128), BF16),
-            vmem((16, 16, 128), BF16),
-            vmem((256, 128), F32),
-            vmem((16, 16, 128), BF16),
-            vmem((16, 16, 128), BF16),
-            vmem((16, 16, 128), BF16),
-            vmem((16, 16, 128), BF16),
-            vmem((256, 128), F32),
-            vmem((16, 16, 128), BF16),
-            vmem((16, 16, 128), BF16),
-            vmem((C, C), F32),
-            vmem((C, C), BF16),
+            vmem((COLS, 16, 256), BF16),
+            vmem((COLS, 16, 256), BF16),
+            pltpu.SemaphoreType.REGULAR,
             dma((5,)),
             dma((16,)),
             dma((16,)),
@@ -370,10 +349,6 @@
             dma((16,)),
             dma((32,)),
             dma((32,)),
-            dma((16,)),
-            dma((16,)),
-            dma((16,)),
-            dma((16,)),
             dma((16,)),
             dma((16,)),
             dma((16,)),

time: 48.3 us -> 45.8 us (0.948)
  Pallas kernels: 46.6 us -> 44.1 us
    pallas_call x1, Pallas kernels: 46.6 us -> 44.1 us  [body(): pl.pallas_call(kernel, out_shape=jax.ShapeDtypeStruct((IL, KL, C), BF16),...]
where the time goes in v3:
time: 45.8 us; the launch traced here: 45.7 us
  Pallas kernels  44.1 us (96%)
  local copies, waits for them, and re-layouts  1.57 us (3%)
    pallas_call x1, Pallas kernels, body(): pl.pallas_call(kernel, out_shape=jax.ShapeDtypeStruct((IL, KL, C), BF16),...  44.1 us
    unnamed x1, local copies, waits for them, and re-layouts  1.57 us

profile of v3, /device:TPU:1, one launch (start us, length us, event | category | flops | bytes accessed | tf_op | source)
XLA Modules:
  0.0 45.7 jit_solution(13220916765334863244)
XLA Ops:
  0.0 44.1 %shard_map.55 = bf16[16,32,128]{2,1,0:T(8,128)(2,1)} custom-call(bf16[16,32,128]{2,1,0:T(8,128)(2,1)} %pair_hbm.1, s32[16,32]{1,0:T(8,128)} %mask_hbm.1, bf16[128,512]{1,0:T(8,128)(2,1)} %w_hbm.1, bf16[128,128]{1,0:T(8,128)(2,1)} %gw_hbm.1, bf16[128,128]{1,0:T(8,128)(2,1)} %ow_hbm.1), custom_call_target="tpu_custom_call" | custom-call | flops 170000000 | bytes 500000 | tf_op jit(solution)/shard_map/pallas_call | solution.py:312
  44.1 1.6 %copy.7 = bf16[16,32,128]{2,1,0:T(8,128)(2,1)} copy(bf16[16,32,128]{2,1,0:T(8,128)(2,1)} %shard_map.55) | data formatting | bytes 262144

commit v4 on v3

--- a/solution.py
+++ b/solution.py
@@ -165,7 +165,7 @@
 
     @pl.loop(0, 31)
     def _(n):
-        g, to = col_peer(n // 2), (xh + 1 - n % 2) % 2
+        g, to = col_peer(n % 16), (xh + 1 - n // 16) % 2
         send(send_r2.at[g], recv_r2.at[xh * 16 + c], sr2.at[n], rr2.at[xh * 16 + c], row(to, z, core), g)
 
     recv_r2[xh * 16 + c] = send_r2[c]

time: 45.8 us -> 44.8 us (0.978)
  Pallas kernels: 44.1 us -> 43 us
    pallas_call x1, Pallas kernels: 44.1 us -> 43 us  [body(): pl.pallas_call(kernel, out_shape=jax.ShapeDtypeStruct((IL, KL, C), BF16),...]
where the time goes in v4:
time: 44.8 us; the launch traced here: 44.6 us
  Pallas kernels  43 us (96%)
  local copies, waits for them, and re-layouts  1.57 us (4%)
    pallas_call x1, Pallas kernels, body(): pl.pallas_call(kernel, out_shape=jax.ShapeDtypeStruct((IL, KL, C), BF16),...  43 us
    unnamed x1, local copies, waits for them, and re-layouts  1.57 us

profile of v4, /device:TPU:1, one launch (start us, length us, event | category | flops | bytes accessed | tf_op | source)
XLA Modules:
  0.0 44.6 jit_solution(2542820004121966911)
XLA Ops:
  0.0 43.0 %shard_map.55 = bf16[16,32,128]{2,1,0:T(8,128)(2,1)} custom-call(bf16[16,32,128]{2,1,0:T(8,128)(2,1)} %pair_hbm.1, s32[16,32]{1,0:T(8,128)} %mask_hbm.1, bf16[128,512]{1,0:T(8,128)(2,1)} %w_hbm.1, bf16[128,128]{1,0:T(8,128)(2,1)} %gw_hbm.1, bf16[128,128]{1,0:T(8,128)(2,1)} %ow_hbm.1), custom_call_target="tpu_custom_call" | custom-call | flops 170000000 | bytes 500000 | tf_op jit(solution)/shard_map/pallas_call | solution.py:312
  43.1 1.6 %copy.7 = bf16[16,32,128]{2,1,0:T(8,128)(2,1)} copy(bf16[16,32,128]{2,1,0:T(8,128)(2,1)} %shard_map.55) | data formatting | bytes 262144

commit v5 on v4

--- a/solution.py
+++ b/solution.py
@@ -163,10 +163,15 @@
 
     pl.semaphore_wait(met, 2)
 
-    @pl.loop(0, 31)
-    def _(n):
-        g, to = col_peer(n % 16), (xh + 1 - n // 16) % 2
-        send(send_r2.at[g], recv_r2.at[xh * 16 + c], sr2.at[n], rr2.at[xh * 16 + c], row(to, z, core), g)
+    @pl.loop(0, 16)
+    def _(n):
+        g = col_peer(n + 1 - 2 * (n % 2))
+        send(send_r2.at[g], recv_r2.at[xh * 16 + c], sr2.at[n], rr2.at[xh * 16 + c], partner, g)
+
+    @pl.loop(0, 15)
+    def _(n):
+        g = col_peer(n)
+        send(send_r2.at[g], recv_r2.at[xh * 16 + c], sr2.at[16 + n], rr2.at[xh * 16 + c], r, g)
 
     recv_r2[xh * 16 + c] = send_r2[c]
 
@@ -214,12 +219,14 @@
     loads[4].wait()
     gate[...] = sigmoid(jnp.dot(normed, gw_ref[...], preferred_element_type=F32)).reshape(IL, KL, C)
 
-    @pl.loop(1, 32)
-    def _(d):
-        m = (xh * 16 + c + d) % 32
-        landed(recv_r2.at[m], rr2.at[m])
-
     for h in range(2):
+
+        @pl.loop(16 * h, 16 * h + 16)
+        def _(m):
+            @pl.when(m != xh * 16 + c)
+            def _():
+                landed(recv_r2.at[m], rr2.at[m])
+
         for a in range(4):
             for b in range(2):
                 tiles = [recv_r2[16 * h + 4 * a + q, :, 128 * b : 128 * b + 128].astype(F32) for q in range(4)]

time: 44.8 us -> 44.6 us (level)
  no operation moved by 1% of the time
where the time goes in v5:
time: 44.6 us; the launch traced here: 44.5 us
  Pallas kernels  42.9 us (96%)
  local copies, waits for them, and re-layouts  1.57 us (4%)
    pallas_call x1, Pallas kernels, body(): pl.pallas_call(kernel, out_shape=jax.ShapeDtypeStruct((IL, KL, C), BF16),...  42.9 us
    unnamed x1, local copies, waits for them, and re-layouts  1.57 us

profile of v5, /device:TPU:1, one launch (start us, length us, event | category | flops | bytes accessed | tf_op | source)
XLA Modules:
  0.0 44.5 jit_solution(13541560188902691619)
XLA Ops:
  0.0 42.9 %shard_map.55 = bf16[16,32,128]{2,1,0:T(8,128)(2,1)} custom-call(bf16[16,32,128]{2,1,0:T(8,128)(2,1)} %pair_hbm.1, s32[16,32]{1,0:T(8,128)} %mask_hbm.1, bf16[128,512]{1,0:T(8,128)(2,1)} %w_hbm.1, bf16[128,128]{1,0:T(8,128)(2,1)} %gw_hbm.1, bf16[128,128]{1,0:T(8,128)(2,1)} %ow_hbm.1), custom_call_target="tpu_custom_call" | custom-call | flops 170000000 | bytes 500000 | tf_op jit(solution)/shard_map/pallas_call | solution.py:319
  42.9 1.6 %copy.7 = bf16[16,32,128]{2,1,0:T(8,128)(2,1)} copy(bf16[16,32,128]{2,1,0:T(8,128)(2,1)} %shard_map.55) | data formatting | bytes 262144

commit v6 on v5

--- a/solution.py
+++ b/solution.py
@@ -251,7 +251,7 @@
 
     @pl.loop(0, 15)
     def _(n):
-        to = zc_peer(n)
+        to = (z + far(n % 8)) % NZ * 2 + (core + 1 - n // 8) % 2
         send(send3.at[to], recv3.at[zc], s3.at[to], r3.at[zc], xh * 16 + to, c)
 
     recv3[zc] = send3[zc]

time: 44.6 us -> 44.7 us (level)
  no operation moved by 1% of the time
where the time goes in v6:
time: 44.7 us; the launch traced here: 44.5 us
  Pallas kernels  42.9 us (96%)
  local copies, waits for them, and re-layouts  1.57 us (4%)
    pallas_call x1, Pallas kernels, body(): pl.pallas_call(kernel, out_shape=jax.ShapeDtypeStruct((IL, KL, C), BF16),...  42.9 us
    unnamed x1, local copies, waits for them, and re-layouts  1.57 us

profile of v6, /device:TPU:1, one launch (start us, length us, event | category | flops | bytes accessed | tf_op | source)
XLA Modules:
  0.0 44.5 jit_solution(1080997031773541232)
XLA Ops:
  0.0 42.9 %shard_map.55 = bf16[16,32,128]{2,1,0:T(8,128)(2,1)} custom-call(bf16[16,32,128]{2,1,0:T(8,128)(2,1)} %pair_hbm.1, s32[16,32]{1,0:T(8,128)} %mask_hbm.1, bf16[128,512]{1,0:T(8,128)(2,1)} %w_hbm.1, bf16[128,128]{1,0:T(8,128)(2,1)} %gw_hbm.1, bf16[128,128]{1,0:T(8,128)(2,1)} %ow_hbm.1), custom_call_target="tpu_custom_call" | custom-call | flops 170000000 | bytes 500000 | tf_op jit(solution)/shard_map/pallas_call | solution.py:319
  43.0 1.6 %copy.7 = bf16[16,32,128]{2,1,0:T(8,128)(2,1)} copy(bf16[16,32,128]{2,1,0:T(8,128)(2,1)} %shard_map.55) | data formatting | bytes 262144

commit v7 on v5

--- a/solution.py
+++ b/solution.py
@@ -73,30 +73,30 @@
     def send(src, dst, ssem, rsem, to_row, to_col):
         pltpu.make_async_remote_copy(src, dst, ssem, rsem, (to_row, to_col), MESH).start()
 
+    barrier = pltpu.get_barrier_semaphore()
+
+    def greet(to_row, to_col):
+        pl.semaphore_signal(barrier, inc=1, device_id=(to_row, to_col), device_id_type=MESH)
+
+    sibling, partner = r + 1 - 2 * core, (r + 16) % ROWS
+
+    @pl.loop(1, COLS)
+    def _(d):
+        greet(r, (c + d) % COLS)
+
+    @pl.loop(1, NZ)
+    def _(d):
+        greet(row(xh, (z + d) % NZ, core), c)
+
+    greet(sibling, c)
+    greet(partner, c)
+
     loads = []
     for n, (src, dst) in enumerate(
         ((pair_hbm, pair_ref), (mask_hbm, mask_ref), (w_hbm, w_ref), (gw_hbm, gw_ref), (ow_hbm, ow_ref))
     ):
         loads.append(pltpu.make_async_copy(src, dst, load_sem.at[n]))
         loads[-1].start()
-
-    barrier = pltpu.get_barrier_semaphore()
-
-    def greet(to_row, to_col):
-        pl.semaphore_signal(barrier, inc=1, device_id=(to_row, to_col), device_id_type=MESH)
-
-    sibling, partner = r + 1 - 2 * core, (r + 16) % ROWS
-
-    @pl.loop(1, COLS)
-    def _(d):
-        greet(r, (c + d) % COLS)
-
-    @pl.loop(1, NZ)
-    def _(d):
-        greet(row(xh, (z + d) % NZ, core), c)
-
-    greet(sibling, c)
-    greet(partner, c)
 
     for load in loads[:2]:
         load.wait()

time: 44.6 us -> 44.7 us (level)
  no operation moved by 1% of the time
where the time goes in v7:
time: 44.7 us; the launch traced here: 44.4 us
  Pallas kernels  42.9 us (96%)
  local copies, waits for them, and re-layouts  1.57 us (4%)
    pallas_call x1, Pallas kernels, body(): pl.pallas_call(kernel, out_shape=jax.ShapeDtypeStruct((IL, KL, C), BF16),...  42.9 us
    unnamed x1, local copies, waits for them, and re-layouts  1.57 us

profile of v7, /device:TPU:1, one launch (start us, length us, event | category | flops | bytes accessed | tf_op | source)
XLA Modules:
  0.0 44.4 jit_solution(4370330689944634398)
XLA Ops:
  0.0 42.9 %shard_map.55 = bf16[16,32,128]{2,1,0:T(8,128)(2,1)} custom-call(bf16[16,32,128]{2,1,0:T(8,128)(2,1)} %pair_hbm.1, s32[16,32]{1,0:T(8,128)} %mask_hbm.1, bf16[128,512]{1,0:T(8,128)(2,1)} %w_hbm.1, bf16[128,128]{1,0:T(8,128)(2,1)} %gw_hbm.1, bf16[128,128]{1,0:T(8,128)(2,1)} %ow_hbm.1), custom_call_target="tpu_custom_call" | custom-call | flops 170000000 | bytes 500000 | tf_op jit(solution)/shard_map/pallas_call | solution.py:319
  42.9 1.6 %copy.7 = bf16[16,32,128]{2,1,0:T(8,128)(2,1)} copy(bf16[16,32,128]{2,1,0:T(8,128)(2,1)} %shard_map.55) | data formatting | bytes 262144
